TPU v7x, 32 devices: a whole 2x2x4 slice. The times are simulated.
32 devices in a mesh: dp: 16 (over z, y, x), feat: 2 (over core).
Axes of the slice: x: 2, y: 2, z: 4, core: 2. Of those that a mesh axis runs over, the one named last changes fastest.
Arguments:
- inputs: float32 [20480, 640], P('dp', 'feat'), may hold values from -6 to 6
- encoder: bfloat16 [20480, 640], P('dp', 'feat'), may hold values from -6 to 6
- output_grad: float32 [20480, 640], P('dp', 'feat'), may hold values from -6 to 6
- target_lengths: int32 [32, 24], P(('dp', 'feat')), may hold values from 0 to 256, as said below
- source_lengths: int32 [32, 24], P(('dp', 'feat')), may hold values from 0 to 256, as said below
- gains: float32 [3, 640], P(None, 'feat'), may hold values from 0.5 to 1.5
- shifts: float32 [3, 640], P(None, 'feat'), may hold values from -2 to 2
- self_inproj: bfloat16 [640, 1920], replicated, may hold values from -0.25 to 0.25
- self_outproj: bfloat16 [640, 640], replicated, may hold values from -1 to 1
- cross_query: bfloat16 [640, 640], replicated, may hold values from -0.25 to 0.25
- cross_keyvalue: bfloat16 [640, 1280], replicated, may hold values from -0.25 to 0.25
- cross_outproj: bfloat16 [640, 640], replicated, may hold values from -1 to 1
- ffn_expand: bfloat16 [640, 3072], replicated, may hold values from -0.25 to 0.25
- ffn_reduce: bfloat16 [3072, 640], replicated, may hold values from -0.109375 to 0.109375
Outputs:
- layer_out: float32 [20480, 640], P('dp', 'feat')
- input_grad: float32 [20480, 640], P('dp', 'feat')
- encoder_grad: float32 [20480, 640], P('dp', 'feat')
- gain_grad: float32 [3, 640], P(None, 'feat')
- shift_grad: float32 [3, 640], P(None, 'feat')
- self_inproj_grad: float32 [640, 1920], P('dp', 'feat')
- self_outproj_grad: float32 [640, 640], P('dp', 'feat')
- cross_query_grad: float32 [640, 640], P('dp', 'feat')
- cross_keyvalue_grad: float32 [640, 1280], P('dp', 'feat')
- cross_outproj_grad: float32 [640, 640], P('dp', 'feat')
- ffn_expand_grad: float32 [640, 3072], P('dp', 'feat')
- ffn_reduce_grad: float32 [3072, 640], P('dp', 'feat')
Inputs may be any that keep to these rules, and one draw needn't show every extreme that they name: `target_lengths`: in each bucket the nonzero lengths fill the first slots and zeros the rest; a bucket's lengths sum to 640 or less; in every draw one bucket, chosen from the seed, has a first sentence of 256. `source_lengths`: nonzero exactly where target_lengths is, and at most the target length.
All inputs are finite; a program needn't handle non-finite values.
Results may differ from a plain program's by a relative error of at most 0.017.
Values may be sent and summed in bfloat16 or wider, within the bound.
A program may use at most 192 MiB of HBM per device.

v0:
```python
import math
import jax
import jax.numpy as jnp
from jax import lax
from jax.sharding import PartitionSpec as P

HEADS = 8
EPSILON = 1e-05
MASKED_SCORE = -1e30


def as_sent(array):

    def short(part):
        return part.astype(jnp.bfloat16) if part.dtype == jnp.float32 else part

    return jax.tree.map(short, array)


def inner(left, right):
    return lax.dot_general(
        left, right, (((0,), (0,)), ((), ())), preferred_element_type=jnp.float32
    )


def backward_product(grad, weight):
    return lax.dot_general(
        grad, weight, (((1,), (1,)), ((), ())), preferred_element_type=jnp.float32
    )


def smooth_gate(values):
    return jax.nn.gelu(values, approximate=True)


def row_sums(first, second):
    return (first, second)


def to_tokens(parts):
    return parts


def to_features(parts):
    return parts


def gather_rows(part):
    return lax.all_to_all(part, "feat", split_axis=0, concat_axis=1, tiled=True)


def spread_rows(part):
    return lax.all_to_all(part, "feat", split_axis=1, concat_axis=0, tiled=True)


def norm_forward(values, gain, shift):
    width = values.shape[1]
    total, squares = row_sums(jnp.sum(values, axis=1), jnp.sum(values * values, axis=1))
    center = total / width
    reciprocal = lax.rsqrt(squares / width - center * center + EPSILON)
    normed = (values - center[:, None]) * reciprocal[:, None]
    return (normed, reciprocal, (normed * gain + shift).astype(jnp.bfloat16))


def norm_backward(grad_normed, normed, reciprocal, gain):
    width = normed.shape[1]
    grad_value = grad_normed.astype(jnp.float32)
    scaled = grad_value * gain
    first, second = row_sums(jnp.sum(scaled, axis=1), jnp.sum(scaled * normed, axis=1))
    grad_input = reciprocal[:, None] * (
        scaled - first[:, None] / width - normed * (second[:, None] / width)
    )
    return (grad_input, jnp.sum(grad_value * normed, axis=0), jnp.sum(grad_value, axis=0))


def sentence_rows(lengths, count):
    slots = jnp.arange(lengths.shape[1], dtype=jnp.int32)
    ends = jnp.sum(
        jnp.where(slots[:, None] <= slots[None, :], lengths[0][:, None], 0), axis=0, dtype=jnp.int32
    )
    positions = jnp.arange(count, dtype=jnp.int32)
    sentence = jnp.sum(
        (ends[None, :] <= positions[:, None]).astype(jnp.int32), axis=1, dtype=jnp.int32
    )
    return (sentence, positions < ends[-1])


def split_heads(values):
    return values.reshape(values.shape[0], HEADS, values.shape[1] // HEADS)


def head_scores(queries, keys, allowed):
    head_size = queries.shape[1] // HEADS
    scores = jnp.einsum(
        "qhd,khd->hqk", split_heads(queries), split_heads(keys), preferred_element_type=jnp.float32
    ) * (1.0 / math.sqrt(head_size))
    return jnp.where(allowed[None, :, :], scores, MASKED_SCORE)


def attend_forward(queries, keys, values, allowed):
    scores = head_scores(queries, keys, allowed)
    largest = jnp.max(scores, axis=-1, keepdims=True)
    expo = jnp.exp(scores - largest)
    total = jnp.sum(expo, axis=-1, keepdims=True)
    weights = expo / total
    mixed = jnp.einsum(
        "hqk,khd->qhd",
        weights.astype(jnp.bfloat16),
        split_heads(values),
        preferred_element_type=jnp.float32,
    )
    log_total = largest[..., 0] + jnp.log(total[..., 0])
    return (mixed.reshape(queries.shape).astype(jnp.bfloat16), log_total)


def attend_backward(queries, keys, values, allowed, log_total, grad_mixed):
    head_size = queries.shape[1] // HEADS
    scale = 1.0 / math.sqrt(head_size)
    weights = jnp.exp(head_scores(queries, keys, allowed) - log_total[..., None])
    grad_heads = split_heads(grad_mixed)
    grad_weights = jnp.einsum(
        "qhd,khd->hqk", grad_heads, split_heads(values), preferred_element_type=jnp.float32
    )
    grad_values = jnp.einsum(
        "hqk,qhd->khd", weights.astype(jnp.bfloat16), grad_heads, preferred_element_type=jnp.float32
    )
    centre = jnp.sum(weights * grad_weights, axis=-1, keepdims=True)
    grad_scores = (weights * (grad_weights - centre)).astype(jnp.bfloat16)
    grad_queries = (
        jnp.einsum(
            "hqk,khd->qhd", grad_scores, split_heads(keys), preferred_element_type=jnp.float32
        )
        * scale
    )
    grad_keys = (
        jnp.einsum(
            "hqk,qhd->khd", grad_scores, split_heads(queries), preferred_element_type=jnp.float32
        )
        * scale
    )
    return (
        grad_queries.reshape(queries.shape),
        grad_keys.reshape(keys.shape),
        grad_values.reshape(values.shape),
    )


def masked_rows(grad, valid):
    return jnp.where(valid[:, None], grad, jnp.zeros_like(grad))


def per_device(
    inputs,
    encoder,
    output_grad,
    target_lengths,
    source_lengths,
    gains,
    shifts,
    self_inproj,
    self_outproj,
    cross_query,
    cross_keyvalue,
    cross_outproj,
    ffn_expand,
    ffn_reduce,
):
    inputs = gather_rows(inputs)
    encoder = gather_rows(encoder)
    output_grad = gather_rows(output_grad)
    gains = lax.all_gather(gains, "feat", axis=1, tiled=True)
    shifts = lax.all_gather(shifts, "feat", axis=1, tiled=True)
    count = inputs.shape[0]
    width = self_outproj.shape[0]
    target_seg, target_valid = sentence_rows(target_lengths, count)
    source_seg, source_valid = sentence_rows(source_lengths, count)
    positions = jnp.arange(count, dtype=jnp.int32)
    keep = target_valid.astype(jnp.float32)[:, None]
    self_mask = (target_seg[:, None] == target_seg[None, :]) & (
        positions[None, :] <= positions[:, None]
    )
    self_mask = self_mask & target_valid[:, None] & target_valid[None, :]
    cross_mask = (
        (target_seg[:, None] == source_seg[None, :]) & target_valid[:, None] & source_valid[None, :]
    )
    normed_one, recip_one, normed_cols = norm_forward(inputs, gains[0], shifts[0])
    (normed1,) = to_tokens((normed_cols,))
    projected = jnp.dot(normed1, self_inproj, preferred_element_type=jnp.float32).astype(
        jnp.bfloat16
    )
    queries = projected[:, :width]
    keys = projected[:, width : 2 * width]
    values = projected[:, 2 * width :]
    attended1, log_one = attend_forward(queries, keys, values, self_mask)
    branch = (jnp.dot(attended1, self_outproj, preferred_element_type=jnp.float32) * keep).astype(
        jnp.bfloat16
    )
    (branch_cols,) = to_features((branch,))
    mid_one = inputs + branch_cols.astype(jnp.float32)
    normed_two, recip_two, normed_cols = norm_forward(mid_one, gains[1], shifts[1])
    normed2, source_rows = to_tokens((normed_cols, encoder))
    cross_queries = jnp.dot(normed2, cross_query, preferred_element_type=jnp.float32).astype(
        jnp.bfloat16
    )
    memory = jnp.dot(source_rows, cross_keyvalue, preferred_element_type=jnp.float32).astype(
        jnp.bfloat16
    )
    attended2, log_two = attend_forward(
        cross_queries, memory[:, :width], memory[:, width:], cross_mask
    )
    branch = (jnp.dot(attended2, cross_outproj, preferred_element_type=jnp.float32) * keep).astype(
        jnp.bfloat16
    )
    (branch_cols,) = to_features((branch,))
    mid_two = mid_one + branch_cols.astype(jnp.float32)
    normed_three, recip_three, normed_cols = norm_forward(mid_two, gains[2], shifts[2])
    (normed3,) = to_tokens((normed_cols,))
    expanded = jnp.dot(normed3, ffn_expand, preferred_element_type=jnp.float32).astype(jnp.bfloat16)
    gated, gate_pull = jax.vjp(smooth_gate, expanded.astype(jnp.float32))
    activated = gated.astype(jnp.bfloat16)
    branch = (jnp.dot(activated, ffn_reduce, preferred_element_type=jnp.float32) * keep).astype(
        jnp.bfloat16
    )
    (branch_cols,) = to_features((branch,))
    layer_out = mid_two + branch_cols.astype(jnp.float32)
    (grad_branch,) = to_tokens((output_grad.astype(jnp.bfloat16),))
    grad_branch = masked_rows(grad_branch, target_valid)
    reduce_grad = inner(activated, grad_branch)
    grad_act = backward_product(grad_branch, ffn_reduce)
    (grad_pre,) = gate_pull(grad_act)
    grad_expanded = grad_pre.astype(jnp.bfloat16)
    expand_grad = inner(normed3, grad_expanded)
    grad_normed = backward_product(grad_expanded, ffn_expand).astype(jnp.bfloat16)
    (grad_cols,) = to_features((grad_normed,))
    part_three, gain_three, shift_three = norm_backward(
        grad_cols, normed_three, recip_three, gains[2]
    )
    grad_mid_two = output_grad + part_three
    (grad_branch,) = to_tokens((grad_mid_two.astype(jnp.bfloat16),))
    grad_branch = masked_rows(grad_branch, target_valid)
    cross_out_grad = inner(attended2, grad_branch)
    grad_attended = backward_product(grad_branch, cross_outproj).astype(jnp.bfloat16)
    grad_cq, grad_ck, grad_cv = attend_backward(
        cross_queries, memory[:, :width], memory[:, width:], cross_mask, log_two, grad_attended
    )
    grad_cq = grad_cq.astype(jnp.bfloat16)
    grad_memory = jnp.concatenate([grad_ck, grad_cv], axis=1).astype(jnp.bfloat16)
    cross_query_grad = inner(normed2, grad_cq)
    cross_kv_grad = inner(source_rows, grad_memory)
    grad_normed = backward_product(grad_cq, cross_query).astype(jnp.bfloat16)
    grad_source = backward_product(grad_memory, cross_keyvalue).astype(jnp.bfloat16)
    grad_cols, grad_source_cols = to_features((grad_normed, grad_source))
    part_two, gain_two, shift_two = norm_backward(grad_cols, normed_two, recip_two, gains[1])
    grad_mid_one = grad_mid_two + part_two
    (grad_branch,) = to_tokens((grad_mid_one.astype(jnp.bfloat16),))
    grad_branch = masked_rows(grad_branch, target_valid)
    self_out_grad = inner(attended1, grad_branch)
    grad_attended = backward_product(grad_branch, self_outproj).astype(jnp.bfloat16)
    grad_q, grad_k, grad_v = attend_backward(
        queries, keys, values, self_mask, log_one, grad_attended
    )
    grad_projected = jnp.concatenate([grad_q, grad_k, grad_v], axis=1).astype(jnp.bfloat16)
    self_in_grad = inner(normed1, grad_projected)
    grad_normed = backward_product(grad_projected, self_inproj).astype(jnp.bfloat16)
    (grad_cols,) = to_features((grad_normed,))
    part_one, gain_one, shift_one = norm_backward(grad_cols, normed_one, recip_one, gains[0])
    input_grad = grad_mid_one + part_one
    gain_local = jnp.stack([gain_one, gain_two, gain_three], axis=0)
    shift_local = jnp.stack([shift_one, shift_two, shift_three], axis=0)
    vectors = lax.psum(jnp.concatenate([gain_local, shift_local], axis=0), ("dp", "feat"))
    half = vectors.shape[1] // lax.axis_size("feat")
    vectors = lax.dynamic_slice_in_dim(vectors, lax.axis_index("feat") * half, half, axis=1)
    gain_grad, shift_grad = (vectors[:3], vectors[3:])
    weight_terms = (
        self_in_grad,
        self_out_grad,
        cross_query_grad,
        cross_kv_grad,
        cross_out_grad,
        expand_grad,
        reduce_grad,
    )
    summed = []
    for term in weight_terms:
        pair = lax.psum_scatter(term.astype(jnp.bfloat16), "feat", scatter_dimension=1, tiled=True)
        summed.append(
            lax.psum_scatter(pair, "dp", scatter_dimension=0, tiled=True).astype(jnp.float32)
        )
    return (
        spread_rows(layer_out),
        spread_rows(input_grad),
        spread_rows(grad_source_cols).astype(jnp.float32),
        gain_grad,
        shift_grad,
        *summed,
    )


def solution(mesh):
    in_specs = (
        P("dp", "feat"),
        P("dp", "feat"),
        P("dp", "feat"),
        P(("dp", "feat"), None),
        P(("dp", "feat"), None),
        P(None, "feat"),
        P(None, "feat"),
        P(),
        P(),
        P(),
        P(),
        P(),
        P(),
        P(),
    )
    out_specs = (
        P("dp", "feat"),
        P("dp", "feat"),
        P("dp", "feat"),
        P(None, "feat"),
        P(None, "feat"),
        P("dp", "feat"),
        P("dp", "feat"),
        P("dp", "feat"),
        P("dp", "feat"),
        P("dp", "feat"),
        P("dp", "feat"),
        P("dp", "feat"),
    )
    return jax.shard_map(
        per_device, mesh=mesh, in_specs=in_specs, out_specs=out_specs, check_vma=False
    )
```

profile of v0, /device:TPU:0, one launch (start us, length us, event | category | flops | bytes accessed | tf_op | source)
XLA Modules:
  0.0 732.3 jit_solution(13034640641992369800)
XLA Ops:
  7.2 2.3 copy.193
  9.5 3.5 all-to-all-start.1
  16.5 2.0 all-gather
  18.6 1.8 all-gather.1
  20.5 2.7 copy.192
  23.2 4.7 all-to-all-start
  27.8 2.9 convolution_convert_fusion.6
  31.8 2.2 copy.144
  35.3 2.7 copy.191
  38.0 4.7 all-to-all-start.3
  46.0 1.7 add_convert_fusion.2
  47.7 2.2 convolution_convert_fusion.4
  51.4 2.2 copy.140
  53.6 2.2 copy.139
  58.6 8.8 %fusion.79 = f32[640,3072]{1,0:T(8,128)} fusion(bf16[640,640]{0,1:T(8,128)(2,1)S(1)} %fusion.60, bf16[3072,640]{1,0:T(8,128)(2,1)} %param.27), kind=kOutput, calls=%fused_computation.178 | convolution fusion | flops 2516582400 | bytes 12615680 | tf_op jit(solution)/shard_map/dot_general | solution.py:27
  68.6 2.5 fusion.77
  71.1 1.7 fusion
  72.9 2.9 copy-done.1
  75.8 3.7 fusion.59
  79.5 2.8 fusion.73
  84.1 2.5 fusion.78
  86.7 2.0 fusion.1
  88.7 2.7 copy-done.2
  91.4 3.8 fusion.58
  97.4 12.5 %fusion.7 = (bf16[640,3072]{1,0:T(8,128)(2,1)S(1)}, bf16[640,3072]{1,0:T(8,128)(2,1)}) fusion(f32[640,3072]{1,0:T(8,128)} %fusion.79, bf16[640,3072]{1,0:T(8,128)(2,1)S(1)} %copy-done.50, f32[640,640]{0,1:T(8,128)S(1)} %get-tuple-element.118, f32[640]{0:T(1024)S(1)} %get-tuple-element.91, f32[640]{0:T(1024)S(1)} %get-tuple-element.130, ...), kind=kOutput, calls=%fused_computation.24 | convolution fusion | flops 2561884160 | bytes 21309440 | tf_op jit(solution)/shard_map/dot_general | solution.py:218
  109.9 3.6 fusion.44
  113.5 2.0 fusion.42
  116.7 1.8 convolution_convert_fusion.12
  118.6 2.6 convolution_convert_fusion.11
  121.3 12.5 %multiply_reduce_fusion.1 = (f32[8,640]{1,0:T(8,128)S(1)}, f32[8,640,640]{1,2,0:T(8,128)}) fusion(f32[8,640,640]{1,2,0:T(8,128)} %copy-done.2, f32[8,640]{1,0:T(8,128)S(1)} %log_add_fusion.1, bf16[640,8,80]{0,2,1:T(8,128)(2,1)S(1)} %bitcast.172, bf16[640,8,80]{0,2,1:T(8,128)(2,1)} %bitcast.186), kind=kOutput, calls=%fused_computation.9 | convolution fusion | flops 534113280 | bytes 27893760 | tf_op jit(solution)/shard_map/qhd,khd->hqk/dot_general | solution.py:121
  133.8 6.6 multiply_convert_fusion.1
  144.1 2.0 convolution_convert_fusion.13
  146.4 3.2 fusion.45
  151.3 1.8 convolution_convert_fusion.14
  153.2 5.6 multiply_convert_fusion.2
  158.8 7.3 fusion.52
  167.0 2.8 fusion.22
  170.1 2.4 convolution_convert_fusion.9
  172.5 12.1 %multiply_reduce_fusion = (f32[8,640]{1,0:T(8,128)S(1)}, f32[8,640,640]{1,2,0:T(8,128)}) fusion(f32[8,640,640]{1,2,0:T(8,128)} %copy-done.1, f32[8,640]{1,0:T(8,128)S(1)} %log_add_fusion, bf16[640,8,80]{0,2,1:T(8,128)(2,1)S(1)} %bitcast.174, bf16[640,8,80]{0,2,1:T(8,128)(2,1)S(1)} %bitcast.184), kind=kOutput, calls=%fused_computation.6 | convolution fusion | flops 534113280 | bytes 27893760 | tf_op jit(solution)/shard_map/qhd,khd->hqk/dot_general | solution.py:121
  185.6 6.6 multiply_convert_fusion
  192.2 2.2 multiply_convert_fusion.3
  195.7 2.2 fusion.55
  198.9 3.9 convolution_convert_fusion.3
  204.0 7.4 %convolution_convert_fusion = bf16[3072,640]{0,1:T(8,128)(2,1)} fusion(bf16[640,640]{0,1:T(8,128)(2,1)S(1)} %copy-done.34, bf16[640,3072]{1,0:T(8,128)(2,1)} %get-tuple-element.120), kind=kOutput, calls=%fused_computation.37 | convolution fusion | flops 2538209280 | bytes 8683520 | tf_op jit(solution)/shard_map/dot_general | solution.py:21
  211.5 8.4 %convolution_convert_fusion.1 = bf16[640,3072]{1,0:T(8,128)(2,1)} fusion(bf16[640,3072]{1,0:T(8,128)(2,1)} %copy-done.55, f32[640,640]{0,1:T(8,128)} %copy-done.18, f32[640]{0:T(1024)S(1)} %get-tuple-element.91, f32[640]{0:T(1024)S(1)} %get-tuple-element.130, f32[640]{0:T(1024)S(1)} %get-tuple-element.108, f32[640]{0:T(1024)S(1)} %get-tuple-element.107), kind=kOutput, calls=%fused_computation.38 | convolution fusion | flops 2520596480 | bytes 9512960 | tf_op jit(solution)/shard_map/dot_general | solution.py:21
  220.7 2.5 copy.170
  223.4 8.2 %reduce-scatter.33.cloned.1.call-done = bf16[3072,320]{0,1:T(8,128)(2,1)} async-done(((bf16[3072,640]{0,1:T(8,128)(2,1)}), bf16[3072,320]{0,1:T(8,128)(2,1)}) %reduce-scatter.33.cloned.1.call-update) | async-done | bytes 1966096 | tf_op jit(solution)/shard_map/reduce_scatter | solution.py:285
  231.6 4.1 copy.180
  235.8 11.1 %reduce-scatter.29.cloned.1.call-done = bf16[640,1536]{1,0:T(8,128)(2,1)} async-done(((bf16[640,3072]{1,0:T(8,128)(2,1)}), bf16[640,1536]{1,0:T(8,128)(2,1)}) %reduce-scatter.29.cloned.1.call-update) | async-done | bytes 1966096 | tf_op jit(solution)/shard_map/reduce_scatter | solution.py:285
  246.9 8.8 %convert_add_fusion.1 = f32[640,640]{0,1:T(8,128)} fusion(f32[640,640]{0,1:T(8,128)} %copy-done.18, bf16[3072,640]{1,0:T(8,128)(2,1)} %param.27, f32[640]{0:T(1024)S(1)} %fusion.61, bf16[640,3072]{1,0:T(8,128)(2,1)} %get-tuple-element.120), kind=kOutput, calls=%fused_computation.93 | convolution fusion | flops 2537881600 | bytes 11143680 | tf_op jit(solution)/shard_map/dot_general | solution.py:221
  255.8 4.8 all-to-all-start.2
  260.6 4.1 convolution_convert_fusion.7
  264.7 4.0 all-to-all-start.5
  268.7 2.9 copy.185
  271.6 4.0 fusion.46
  275.7 3.2 fusion.34
  278.9 4.7 all-to-all-start.4
  286.2 2.7 copy.186
  290.2 40.8 %psum.7 = f32[6,640]{1,0:T(8,128)S(1)} all-reduce(f32[6,640]{1,0:T(8,128)S(1)} %concatenate.13), channel_id=1, replica_groups=mesh['dp'=16,'feat'=2] {'dp','feat'}, use_global_device_ids=true, to_apply=%region_28.29 | all-reduce | flops 3840 | bytes 30720 | tf_op jit(solution)/shard_map/psum | solution.py:270
  331.7 50.3 %all-reduce.7.cloned.1.call-done = (bf16[640,320]{0,1:T(8,128)(2,1)}, bf16[640,320]{0,1:T(8,128)(2,1)}, bf16[640,640]{0,1:T(8,128)(2,1)}, bf16[640,320]{0,1:T(8,128)(2,1)}) async-done(((bf16[640,320]{0,1:T(8,128)(2,1)}, bf16[640,320]{0,1:T(8,128)(2,1)}, bf16[640,640]{0,1:T(8,128)(2,1)}, bf16[640,320]{0,1:T(8,128)(2,1)}), (bf16[640,320]{0,1:T(8,128)(2,1)}, bf16[640,320]{0,1:T(8,128)(2,1)}, ...) | async-done | bytes 2048016
  389.1 73.2 %reduce-scatter.35.cloned.1.call-done = bf16[40,960]{1,0:T(8,128)(2,1)} async-done(((bf16[640,960]{1,0:T(8,128)(2,1)}), bf16[40,960]{1,0:T(8,128)(2,1)}) %reduce-scatter.35.cloned.1.call-update) | async-done | bytes 76816
  464.1 127.7 %reduce-scatter.37.cloned.1.call-done = bf16[192,320]{1,0:T(8,128)(2,1)} async-done(((bf16[3072,320]{1,0:T(8,128)(2,1)}), bf16[192,320]{1,0:T(8,128)(2,1)}) %reduce-scatter.37.cloned.1.call-update) | async-done | bytes 122896
  593.7 129.9 %reduce-scatter.31.cloned.1.call-done = bf16[40,1536]{1,0:T(8,128)(2,1)} async-done(((bf16[640,1536]{1,0:T(8,128)(2,1)}), bf16[40,1536]{1,0:T(8,128)(2,1)}) %reduce-scatter.31.cloned.1.call-update) | async-done | bytes 122896 | tf_op jit(solution)/shard_map/reduce_scatter | solution.py:287
  723.6 1.6 convert_element_type.259
  (221 shorter events, 46.7 us)
Async XLA Ops:
  7.2 40.5 %copy-start = (bf16[640,1920]{1,0:T(8,128)(2,1)S(1)}, bf16[640,1920]{1,0:T(8,128)(2,1)}, u32[]{:S(2)}) copy-start(bf16[640,1920]{1,0:T(8,128)(2,1)} %param.21) | copy-start | bytes 7372804
  7.2 5.8 copy-start.52
  7.2 7.8 %copy-start.53 = (s32[1,24]{1,0:T(1,128)S(1)}, s32[1,24]{1,0:T(1,128)}, u32[]{:S(2)}) copy-start(s32[1,24]{1,0:T(1,128)} %param.18) | copy-start | bytes 292
  7.2 9.3 %copy-start.48 = (f32[3,320]{1,0:T(4,128)S(1)}, f32[3,320]{1,0:T(4,128)}, u32[]{:S(2)}) copy-start(f32[3,320]{1,0:T(4,128)} %param.19) | copy-start | bytes 11524
  7.2 11.3 %copy-start.49 = (f32[3,320]{1,0:T(4,128)S(1)}, f32[3,320]{1,0:T(4,128)}, u32[]{:S(2)}) copy-start(f32[3,320]{1,0:T(4,128)} %param.20) | copy-start | bytes 11524
  9.5 13.7 %all-to-all-start.1 = ((bf16[2,640,320]{1,2,0:T(8,128)(2,1)}), bf16[2,640,320]{1,2,0:T(8,128)(2,1)S(1)}, u32[]{:S(2)}, u32[]{:S(2)}) async-start(bf16[2,640,320]{1,2,0:T(8,128)(2,1)} %bitcast.161), calls=%async_computation.1 | async-start | bytes 1638400 | tf_op jit(solution)/shard_map/all_to_all | solution.py:49
  23.2 4.7 copy-start.29
  23.2 14.9 %all-to-all-start = ((f32[2,640,320]{1,2,0:T(8,128)}), f32[2,640,320]{1,2,0:T(8,128)}, u32[]{:S(2)}, u32[]{:S(2)}) async-start(f32[2,640,320]{1,2,0:T(8,128)} %bitcast.177), calls=%async_computation | async-start | bytes 3276800 | tf_op jit(solution)/shard_map/all_to_all | solution.py:49
  38.0 8.0 %copy-start.42 = (f32[640]{0:T(1024)}, f32[640]{0:T(1024)S(1)}, u32[]{:S(2)}) copy-start(f32[640]{0:T(1024)S(1)} %get-tuple-element.128) | copy-start | bytes 7684
  38.0 19.0 %all-to-all-start.3 = ((f32[2,640,320]{1,2,0:T(8,128)}), f32[2,640,320]{1,2,0:T(8,128)}, u32[]{:S(2)}, u32[]{:S(2)}) async-start(f32[2,640,320]{1,2,0:T(8,128)} %bitcast.176), calls=%async_computation.3 | async-start | bytes 3276800 | tf_op jit(solution)/shard_map/all_to_all | solution.py:49
  42.7 177.3 %reduce-scatter.27.cloned.1.call-start = ((), (), s32[]{:S(2)}) async-start(), calls=%async_computation.20 | async-start | bytes 1228800 | tf_op jit(solution)/shard_map/reduce_scatter | solution.py:285
  45.9 4.0 copy-start.44
  46.0 4.0 copy-start.46
  58.6 8.8 %copy-start.33 = (bf16[640,640]{0,1:T(8,128)(2,1)}, bf16[640,640]{0,1:T(8,128)(2,1)S(1)}, u32[]{:S(2)}) copy-start(bf16[640,640]{0,1:T(8,128)(2,1)S(1)} %fusion.60) | copy-start | bytes 2457604
  58.6 10.0 %copy-start.12 = (bf16[640,640]{0,1:T(8,128)(2,1)S(1)}, bf16[640,640]{0,1:T(8,128)(2,1)}, u32[]{:S(2)}) copy-start(bf16[640,640]{0,1:T(8,128)(2,1)} %copy.140) | copy-start | bytes 2457604
  58.6 10.0 %copy-start.16 = (bf16[640,640]{0,1:T(8,128)(2,1)S(1)}, bf16[640,640]{0,1:T(8,128)(2,1)}, u32[]{:S(2)}) copy-start(bf16[640,640]{0,1:T(8,128)(2,1)} %copy.139) | copy-start | bytes 2457604
  71.1 4.7 copy-start.1
  75.8 3.7 copy-start.20
  83.5 3.2 copy-start.25
  86.7 4.7 copy-start.2
  91.4 3.8 copy-start.9
  91.4 3.8 copy-start.19
  96.4 17.2 %copy-start.18 = (f32[640,640]{0,1:T(8,128)}, f32[640,640]{0,1:T(8,128)S(1)}, u32[]{:S(2)}) copy-start(f32[640,640]{0,1:T(8,128)S(1)} %get-tuple-element.118) | copy-start | bytes 4915204
  109.9 3.6 copy-start.55
  118.6 101.5 %reduce-scatter.23.cloned.1.call-start = ((), (), s32[]{:S(2)}) async-start(), calls=%async_computation.18 | async-start | bytes 1228800 | tf_op jit(solution)/shard_map/reduce_scatter | solution.py:285
  121.2 12.6 %slice-start.4 = ((s8[13107200]{0:T(1024)(128)(4,1)}), s8[4194304]{0:T(1024)(128)(4,1)S(1)}, s32[]{:S(2)}) async-start(s8[13107200]{0:T(1024)(128)(4,1)} %bitcast.164), calls=%async_computation.31 | async-start | bytes 8388608
  121.2 12.5 %slice-start.5 = ((s8[13107200]{0:T(1024)(128)(4,1)}), s8[4194304]{0:T(1024)(128)(4,1)S(1)}, s32[]{:S(2)}) async-start(s8[13107200]{0:T(1024)(128)(4,1)} %bitcast.164), calls=%async_computation.32 | async-start | bytes 8388608
  121.2 12.5 %slice-start.6 = ((s8[13107200]{0:T(1024)(128)(4,1)}), s8[4194304]{0:T(1024)(128)(4,1)S(1)}, s32[]{:S(2)}) async-start(s8[13107200]{0:T(1024)(128)(4,1)} %bitcast.164), calls=%async_computation.33 | async-start | bytes 8388608
  121.2 12.5 %slice-start.7 = ((s8[13107200]{0:T(1024)(128)(4,1)}), s8[524288]{0:T(1024)(128)(4,1)S(1)}, s32[]{:S(2)}) async-start(s8[13107200]{0:T(1024)(128)(4,1)} %bitcast.164), calls=%async_computation.34 | async-start | bytes 1048576
  133.8 6.6 copy-start.15
  140.4 3.7 copy-start.10
  146.1 73.9 %reduce-scatter.21.cloned.1.call-start = ((), (), s32[]{:S(2)}) async-start(), calls=%async_computation.17 | async-start | bytes 1228800 | tf_op jit(solution)/shard_map/reduce_scatter | solution.py:285
  146.3 3.2 copy-start.7
  146.3 3.2 copy-start.11
  153.1 66.9 %reduce-scatter.25.cloned.1.call-start = ((), (), s32[]{:S(2)}) async-start(), calls=%async_computation.19 | async-start | bytes 2457600 | tf_op jit(solution)/shard_map/reduce_scatter | solution.py:285
  158.8 7.3 copy-start.35
  158.8 8.2 %copy-start.30 = (bf16[2,640,320]{1,2,0:T(8,128)(2,1)S(1)}, bf16[2,640,320]{1,2,0:T(8,128)(2,1)}, u32[]{:S(2)}) copy-start(bf16[2,640,320]{1,2,0:T(8,128)(2,1)} %copy-done.29) | copy-start | bytes 2457604
  167.0 3.1 copy-start.21
  169.8 51.0 %reduce-scatter.19.cloned.1.call-start = ((), (), s32[]{:S(2)}) async-start(), calls=%async_computation.16 | async-start | bytes 3686400 | tf_op jit(solution)/shard_map/reduce_scatter | solution.py:285
  172.5 12.1 %slice-start = ((s8[13107200]{0:T(1024)(128)(4,1)}), s8[4194304]{0:T(1024)(128)(4,1)S(1)}, s32[]{:S(2)}) async-start(s8[13107200]{0:T(1024)(128)(4,1)} %bitcast.162), calls=%async_computation.27 | async-start | bytes 8388608
  172.5 12.1 %slice-start.1 = ((s8[13107200]{0:T(1024)(128)(4,1)}), s8[4194304]{0:T(1024)(128)(4,1)S(1)}, s32[]{:S(2)}) async-start(s8[13107200]{0:T(1024)(128)(4,1)} %bitcast.162), calls=%async_computation.28 | async-start | bytes 8388608
  172.5 12.9 %slice-start.2 = ((s8[13107200]{0:T(1024)(128)(4,1)}), s8[4194304]{0:T(1024)(128)(4,1)S(1)}, s32[]{:S(2)}) async-start(s8[13107200]{0:T(1024)(128)(4,1)} %bitcast.162), calls=%async_computation.29 | async-start | bytes 8388608
  172.5 13.1 %slice-start.3 = ((s8[13107200]{0:T(1024)(128)(4,1)}), s8[524288]{0:T(1024)(128)(4,1)S(1)}, s32[]{:S(2)}) async-start(s8[13107200]{0:T(1024)(128)(4,1)} %bitcast.162), calls=%async_computation.30 | async-start | bytes 1048576
  185.6 6.6 copy-start.17
  194.4 3.6 copy-start.38
  195.7 3.2 copy-start.32
  202.8 28.7 %reduce-scatter.33.cloned.1.call-start = ((), (), s32[]{:S(2)}) async-start(), calls=%async_computation.23 | async-start | bytes 5898240 | tf_op jit(solution)/shard_map/reduce_scatter | solution.py:285
  211.4 35.5 %reduce-scatter.29.cloned.1.call-start = ((), (), s32[]{:S(2)}) async-start(), calls=%async_computation.21 | async-start | bytes 5898240 | tf_op jit(solution)/shard_map/reduce_scatter | solution.py:285
  219.9 162.0 %all-reduce.7.cloned.1.call-start = ((), (), s32[]{:S(2)}) async-start(), calls=%async_computation.26 | async-start | bytes 4096000
  220.7 241.6 %reduce-scatter.35.cloned.1.call-start = ((), (), s32[]{:S(2)}) async-start(), calls=%async_computation.24 | async-start | bytes 1392640
  223.3 368.5 %reduce-scatter.37.cloned.1.call-start = ((), (), s32[]{:S(2)}) async-start(), calls=%async_computation.25 | async-start | bytes 2506752
  235.7 487.9 %reduce-scatter.31.cloned.1.call-start = ((), (), s32[]{:S(2)}) async-start(), calls=%async_computation.22 | async-start | bytes 2088960 | tf_op jit(solution)/shard_map/reduce_scatter | solution.py:287
  255.8 4.8 copy-start.36
  255.8 8.9 %all-to-all-start.2 = ((f32[640,2,320]{0,2,1:T(8,128)}), f32[640,2,320]{0,2,1:T(8,128)}, u32[]{:S(2)}, u32[]{:S(2)}) async-start(f32[640,2,320]{0,2,1:T(8,128)} %bitcast.198), calls=%async_computation.2 | async-start | bytes 3276800 | tf_op jit(solution)/shard_map/all_to_all | solution.py:53
  264.6 6.9 copy-start.43
  264.6 6.9 copy-start.45
  264.6 6.9 copy-start.47
  264.7 14.2 %all-to-all-start.5 = ((bf16[640,2,320]{0,2,1:T(8,128)(2,1)}), bf16[640,2,320]{0,2,1:T(8,128)(2,1)S(1)}, u32[]{:S(2)}, u32[]{:S(2)}) async-start(bf16[640,2,320]{0,2,1:T(8,128)(2,1)} %bitcast.202), calls=%async_computation.5 | async-start | bytes 1638400 | tf_op jit(solution)/shard_map/all_to_all | solution.py:53
  268.6 2.9 copy-start.27
  268.6 2.9 copy-start.39
  268.7 2.9 copy-start.41
  271.6 4.1 copy-start.5
  278.9 7.3 all-to-all-start.4
  285.0 4.0 copy-start.54
  (17 other events, 30.8 us)
Sparse Core Ops, SparseCore 0:
  118.7 11.1 reduce-scatter.26
  146.2 11.1 reduce-scatter.22
  159.7 9.4 reduce-scatter.20
  171.9 10.2 reduce-scatter.24
  203.0 13.2 reduce-scatter.18
  218.4 13.0 reduce-scatter.32
  233.8 13.0 reduce-scatter.28
  253.9 128.0 all-reduce.6
  384.2 77.9 reduce-scatter.34
  467.0 124.7 reduce-scatter.36
  597.4 126.1 reduce-scatter.30
where the time goes:
time: 742 us; the launch traced here: 732 us
  waiting for transfers between devices  402 us (54%)
  matrix products  145 us (20%)
  local copies, waits for them, and re-layouts  58 us (8%)
  blocking collectives  44.6 us (6%)
  other arithmetic  38.3 us (5%)
  starting transfers between devices  27.4 us (4%)
  between operations  16.2 us (2%)
    unnamed x14, waiting for transfers between devices  252 us
    reduce_scatter x1, waiting for transfers between devices, per_device(): lax.psum_scatter(pair, 'dp', scatter_dimension=0, tiled=True)  130 us
    psum x1, blocking collectives, per_device(): lax.psum(jnp.concatenate([gain_local, shift_local], axis=0), ('dp', 'feat'))  40.8 us
    unnamed x141, local copies, waits for them, and re-layouts  30 us
    dot_general x7, matrix products, backward_product(): lax.dot_general(grad, weight, (((1,), (1,)), ((), ())), preferred_element...  28.6 us
    dot_general x7, matrix products, inner(): lax.dot_general(left, right, (((0,), (0,)), ((), ())), preferred_element_...  28.2 us
    dot_general x2, matrix products, attend_backward(): jnp.einsum('qhd,khd->hqk', grad_heads, split_heads(values), preferred_ele...  24.6 us
    reduce_scatter x7, waiting for transfers between devices, per_device(): lax.psum_scatter(term.astype(jnp.bfloat16), 'feat', scatter_dimension=1,...  19.4 us
  transfers between devices with their start and end apart: 17, of which 7 were waited for; matrix products, arithmetic and copies ran while one was open for 23% of the time, Pallas kernels for 0%

commit v1 on v0

--- a/solution.py
+++ b/solution.py
@@ -3,6 +3,7 @@
 import jax.numpy as jnp
 from jax import lax
 from jax.sharding import PartitionSpec as P
+from jax.lax import all_to_all, axis_size
 
 HEADS = 8
 EPSILON = 1e-05
@@ -50,7 +51,9 @@
 
 
 def spread_rows(part):
-    return lax.all_to_all(part, "feat", split_axis=1, concat_axis=0, tiled=True)
+    return jnp.concatenate(
+        all_to_all(jnp.stack(jnp.split(part, axis_size("feat"), 1), axis=0), "feat", 0, 0), 0
+    )
 
 
 def norm_forward(values, gain, shift):

time: 742 us -> 742 us (level)
    reduce_scatter x7, waiting for transfers between devices: 19.4 us -> 10.6 us  [per_device(): lax.psum_scatter(term.astype(jnp.bfloat16), 'feat', scatter_dimension=1,...]
  transfers between devices with their start and end apart: 17 -> 17, of which waited for: 7 -> 7; matrix products, arithmetic and copies ran while one was open for 23% -> 24% of each run, Pallas kernels for 0% -> 0%
where the time goes in v1:
time: 742 us; the launch traced here: 732 us
  waiting for transfers between devices  400 us (54%)
  matrix products  144 us (19%)
  local copies, waits for them, and re-layouts  59.6 us (8%)
  blocking collectives  44.6 us (6%)
  other arithmetic  40.6 us (5%)
  starting transfers between devices  27.3 us (4%)
  between operations  16.2 us (2%)
    unnamed x14, waiting for transfers between devices  258 us
    reduce_scatter x1, waiting for transfers between devices, per_device(): lax.psum_scatter(pair, 'dp', scatter_dimension=0, tiled=True)  130 us
    psum x1, blocking collectives, per_device(): lax.psum(jnp.concatenate([gain_local, shift_local], axis=0), ('dp', 'feat'))  40.8 us
    unnamed x141, local copies, waits for them, and re-layouts  29.9 us
    dot_general x7, matrix products, inner(): lax.dot_general(left, right, (((0,), (0,)), ((), ())), preferred_element_...  28.1 us
    dot_general x7, matrix products, backward_product(): lax.dot_general(grad, weight, (((1,), (1,)), ((), ())), preferred_element...  27.6 us
    dot_general x2, matrix products, attend_backward(): jnp.einsum('qhd,khd->hqk', grad_heads, split_heads(values), preferred_ele...  24.6 us
  transfers between devices with their start and end apart: 17, of which 7 were waited for; matrix products, arithmetic and copies ran while one was open for 24% of the time, Pallas kernels for 0%

profile of v1, /device:TPU:0, one launch (start us, length us, event | category | flops | bytes accessed | tf_op | source)
XLA Modules:
  0.0 732.4 jit_solution(10152509889014786118)
XLA Ops:
  7.2 2.3 copy.190
  9.5 3.5 all-to-all-start.1
  16.5 2.0 all-gather
  18.6 1.8 all-gather.1
  20.5 2.7 copy.189
  23.2 4.7 all-to-all-start
  27.8 2.9 convolution_convert_fusion.6
  31.8 2.2 copy.141
  35.3 2.7 copy.188
  38.0 4.7 all-to-all-start.3
  46.0 1.7 add_convert_fusion.2
  47.7 2.2 convolution_convert_fusion.4
  51.4 2.2 copy.137
  53.5 2.2 copy.136
  58.6 8.8 %fusion.79 = f32[640,3072]{1,0:T(8,128)} fusion(bf16[640,640]{0,1:T(8,128)(2,1)S(1)} %fusion.60, bf16[3072,640]{1,0:T(8,128)(2,1)} %param.27), kind=kOutput, calls=%fused_computation.187 | convolution fusion | flops 2516582400 | bytes 12615680 | tf_op jit(solution)/shard_map/dot_general | solution.py:28
  68.6 2.5 fusion.77
  71.2 1.7 fusion
  72.9 2.9 copy-done.1
  75.8 3.7 fusion.59
  79.6 2.8 fusion.73
  84.2 2.5 fusion.78
  86.7 2.0 fusion.1
  88.7 2.7 copy-done.2
  91.4 3.8 fusion.58
  97.5 12.5 %fusion.7 = (bf16[640,3072]{1,0:T(8,128)(2,1)S(1)}, bf16[640,3072]{1,0:T(8,128)(2,1)}) fusion(f32[640,3072]{1,0:T(8,128)} %fusion.79, bf16[640,3072]{1,0:T(8,128)(2,1)S(1)} %copy-done.50, f32[640,640]{0,1:T(8,128)S(1)} %get-tuple-element.124, f32[640]{0:T(1024)S(1)} %get-tuple-element.91, f32[640]{0:T(1024)S(1)} %get-tuple-element.136, ...), kind=kOutput, calls=%fused_computation.24 | convolution fusion | flops 2561884160 | bytes 21309440 | tf_op jit(solution)/shard_map/dot_general | solution.py:221
  110.0 3.6 fusion.44
  113.6 2.0 fusion.42
  116.7 1.8 convolution_convert_fusion.12
  118.7 2.6 convolution_convert_fusion.11
  121.3 12.5 %multiply_reduce_fusion.1 = (f32[8,640]{1,0:T(8,128)S(1)}, f32[8,640,640]{1,2,0:T(8,128)}) fusion(f32[8,640,640]{1,2,0:T(8,128)} %copy-done.2, f32[8,640]{1,0:T(8,128)S(1)} %log_add_fusion.1, bf16[640,8,80]{0,2,1:T(8,128)(2,1)S(1)} %bitcast.178, bf16[640,8,80]{0,2,1:T(8,128)(2,1)} %bitcast.191), kind=kOutput, calls=%fused_computation.9 | convolution fusion | flops 534113280 | bytes 27893760 | tf_op jit(solution)/shard_map/qhd,khd->hqk/dot_general | solution.py:124
  133.8 6.6 multiply_convert_fusion.1
  144.1 2.0 convolution_convert_fusion.13
  146.3 3.2 fusion.45
  151.3 1.8 convolution_convert_fusion.14
  153.1 5.6 multiply_convert_fusion.2
  158.7 7.3 fusion.52
  166.9 2.8 fusion.22
  170.0 2.4 convolution_convert_fusion.9
  172.5 12.1 %multiply_reduce_fusion = (f32[8,640]{1,0:T(8,128)S(1)}, f32[8,640,640]{1,2,0:T(8,128)}) fusion(f32[8,640,640]{1,2,0:T(8,128)} %copy-done.1, f32[8,640]{1,0:T(8,128)S(1)} %log_add_fusion, bf16[640,8,80]{0,2,1:T(8,128)(2,1)S(1)} %bitcast.180, bf16[640,8,80]{0,2,1:T(8,128)(2,1)S(1)} %bitcast.189), kind=kOutput, calls=%fused_computation.6 | convolution fusion | flops 534113280 | bytes 27893760 | tf_op jit(solution)/shard_map/qhd,khd->hqk/dot_general | solution.py:124
  185.5 6.6 multiply_convert_fusion
  192.1 2.2 multiply_convert_fusion.3
  195.7 2.2 fusion.55
  198.8 3.9 convolution_convert_fusion.3
  203.9 7.4 %convolution_convert_fusion = bf16[3072,640]{0,1:T(8,128)(2,1)} fusion(bf16[640,640]{0,1:T(8,128)(2,1)S(1)} %copy-done.34, bf16[640,3072]{1,0:T(8,128)(2,1)} %get-tuple-element.126), kind=kOutput, calls=%fused_computation.37 | convolution fusion | flops 2538209280 | bytes 8683520 | tf_op jit(solution)/shard_map/dot_general | solution.py:22
  211.4 8.4 %convolution_convert_fusion.1 = bf16[640,3072]{1,0:T(8,128)(2,1)} fusion(bf16[640,3072]{1,0:T(8,128)(2,1)} %copy-done.55, f32[640,640]{0,1:T(8,128)} %copy-done.18, f32[640]{0:T(1024)S(1)} %get-tuple-element.91, f32[640]{0:T(1024)S(1)} %get-tuple-element.136, f32[640]{0:T(1024)S(1)} %get-tuple-element.114, f32[640]{0:T(1024)S(1)} %get-tuple-element.113), kind=kOutput, calls=%fused_computation.38 | convolution fusion | flops 2520596480 | bytes 9512960 | tf_op jit(solution)/shard_map/dot_general | solution.py:22
  220.7 2.5 copy.167
  223.3 8.2 %reduce-scatter.33.cloned.1.call-done = bf16[3072,320]{0,1:T(8,128)(2,1)} async-done(((bf16[3072,640]{0,1:T(8,128)(2,1)}), bf16[3072,320]{0,1:T(8,128)(2,1)}) %reduce-scatter.33.cloned.1.call-update) | async-done | bytes 1966096 | tf_op jit(solution)/shard_map/reduce_scatter | solution.py:288
  231.5 4.1 copy.177
  235.7 8.8 %convert_add_fusion.1 = f32[640,640]{0,1:T(8,128)} fusion(f32[640,640]{0,1:T(8,128)} %copy-done.18, bf16[3072,640]{1,0:T(8,128)(2,1)} %param.27, f32[640]{0:T(1024)S(1)} %fusion.61, bf16[640,3072]{1,0:T(8,128)(2,1)} %get-tuple-element.126), kind=kOutput, calls=%fused_computation.95 | convolution fusion | flops 2537881600 | bytes 11143680 | tf_op jit(solution)/shard_map/dot_general | solution.py:224
  244.5 2.3 reduce-scatter.29.cloned.1.call-done
  249.6 5.1 all-to-all-start.2
  254.7 3.1 convolution_convert_fusion.7
  258.9 3.6 all-to-all-start.5
  262.5 2.9 copy.182
  265.4 4.0 fusion.46
  269.5 2.0 fusion.34
  272.9 4.7 all-to-all-start.4
  280.2 2.7 copy.183
  284.2 40.8 %psum.7 = f32[6,640]{1,0:T(8,128)S(1)} all-reduce(f32[6,640]{1,0:T(8,128)S(1)} %concatenate.13), channel_id=1, replica_groups=mesh['dp'=16,'feat'=2] {'dp','feat'}, use_global_device_ids=true, to_apply=%region_28.29 | all-reduce | flops 3840 | bytes 30720 | tf_op jit(solution)/shard_map/psum | solution.py:273
  325.7 56.5 %all-reduce.7.cloned.1.call-done = (bf16[640,320]{0,1:T(8,128)(2,1)}, bf16[640,320]{0,1:T(8,128)(2,1)}, bf16[640,640]{0,1:T(8,128)(2,1)}, bf16[640,320]{0,1:T(8,128)(2,1)}) async-done(((bf16[640,320]{0,1:T(8,128)(2,1)}, bf16[640,320]{0,1:T(8,128)(2,1)}, bf16[640,640]{0,1:T(8,128)(2,1)}, bf16[640,320]{0,1:T(8,128)(2,1)}), (bf16[640,320]{0,1:T(8,128)(2,1)}, bf16[640,320]{0,1:T(8,128)(2,1)}, ...) | async-done | bytes 2048016
  389.3 73.2 %reduce-scatter.35.cloned.1.call-done = bf16[40,960]{1,0:T(8,128)(2,1)} async-done(((bf16[640,960]{1,0:T(8,128)(2,1)}), bf16[40,960]{1,0:T(8,128)(2,1)}) %reduce-scatter.35.cloned.1.call-update) | async-done | bytes 76816
  464.3 127.7 %reduce-scatter.37.cloned.1.call-done = bf16[192,320]{1,0:T(8,128)(2,1)} async-done(((bf16[3072,320]{1,0:T(8,128)(2,1)}), bf16[192,320]{1,0:T(8,128)(2,1)}) %reduce-scatter.37.cloned.1.call-update) | async-done | bytes 122896
  593.9 129.9 %reduce-scatter.31.cloned.1.call-done = bf16[40,1536]{1,0:T(8,128)(2,1)} async-done(((bf16[640,1536]{1,0:T(8,128)(2,1)}), bf16[40,1536]{1,0:T(8,128)(2,1)}) %reduce-scatter.31.cloned.1.call-update) | async-done | bytes 122896 | tf_op jit(solution)/shard_map/reduce_scatter | solution.py:290
  723.8 1.6 convert_element_type.255
  (227 shorter events, 51.9 us)
Async XLA Ops:
  7.2 40.5 %copy-start = (bf16[640,1920]{1,0:T(8,128)(2,1)S(1)}, bf16[640,1920]{1,0:T(8,128)(2,1)}, u32[]{:S(2)}) copy-start(bf16[640,1920]{1,0:T(8,128)(2,1)} %param.21) | copy-start | bytes 7372804
  7.2 5.8 copy-start.52
  7.2 7.8 %copy-start.53 = (s32[1,24]{1,0:T(1,128)S(1)}, s32[1,24]{1,0:T(1,128)}, u32[]{:S(2)}) copy-start(s32[1,24]{1,0:T(1,128)} %param.18) | copy-start | bytes 292
  7.2 9.3 %copy-start.48 = (f32[3,320]{1,0:T(4,128)S(1)}, f32[3,320]{1,0:T(4,128)}, u32[]{:S(2)}) copy-start(f32[3,320]{1,0:T(4,128)} %param.19) | copy-start | bytes 11524
  7.2 11.3 %copy-start.49 = (f32[3,320]{1,0:T(4,128)S(1)}, f32[3,320]{1,0:T(4,128)}, u32[]{:S(2)}) copy-start(f32[3,320]{1,0:T(4,128)} %param.20) | copy-start | bytes 11524
  9.5 13.7 %all-to-all-start.1 = ((bf16[2,640,320]{1,2,0:T(8,128)(2,1)}), bf16[2,640,320]{1,2,0:T(8,128)(2,1)S(1)}, u32[]{:S(2)}, u32[]{:S(2)}) async-start(bf16[2,640,320]{1,2,0:T(8,128)(2,1)} %bitcast.167), calls=%async_computation.1 | async-start | bytes 1638400 | tf_op jit(solution)/shard_map/all_to_all | solution.py:50
  23.2 4.7 copy-start.29
  23.2 14.9 %all-to-all-start = ((f32[2,640,320]{1,2,0:T(8,128)}), f32[2,640,320]{1,2,0:T(8,128)}, u32[]{:S(2)}, u32[]{:S(2)}) async-start(f32[2,640,320]{1,2,0:T(8,128)} %bitcast.183), calls=%async_computation | async-start | bytes 3276800 | tf_op jit(solution)/shard_map/all_to_all | solution.py:50
  38.0 8.0 %copy-start.42 = (f32[640]{0:T(1024)}, f32[640]{0:T(1024)S(1)}, u32[]{:S(2)}) copy-start(f32[640]{0:T(1024)S(1)} %get-tuple-element.134) | copy-start | bytes 7684
  38.0 19.0 %all-to-all-start.3 = ((f32[2,640,320]{1,2,0:T(8,128)}), f32[2,640,320]{1,2,0:T(8,128)}, u32[]{:S(2)}, u32[]{:S(2)}) async-start(f32[2,640,320]{1,2,0:T(8,128)} %bitcast.182), calls=%async_computation.3 | async-start | bytes 3276800 | tf_op jit(solution)/shard_map/all_to_all | solution.py:50
  42.7 177.2 %reduce-scatter.27.cloned.1.call-start = ((), (), s32[]{:S(2)}) async-start(), calls=%async_computation.20 | async-start | bytes 1228800 | tf_op jit(solution)/shard_map/reduce_scatter | solution.py:288
  45.9 4.0 copy-start.44
  46.0 4.0 copy-start.46
  58.6 8.8 %copy-start.33 = (bf16[640,640]{0,1:T(8,128)(2,1)}, bf16[640,640]{0,1:T(8,128)(2,1)S(1)}, u32[]{:S(2)}) copy-start(bf16[640,640]{0,1:T(8,128)(2,1)S(1)} %fusion.60) | copy-start | bytes 2457604
  58.6 10.0 %copy-start.12 = (bf16[640,640]{0,1:T(8,128)(2,1)S(1)}, bf16[640,640]{0,1:T(8,128)(2,1)}, u32[]{:S(2)}) copy-start(bf16[640,640]{0,1:T(8,128)(2,1)} %copy.137) | copy-start | bytes 2457604
  58.6 10.0 %copy-start.16 = (bf16[640,640]{0,1:T(8,128)(2,1)S(1)}, bf16[640,640]{0,1:T(8,128)(2,1)}, u32[]{:S(2)}) copy-start(bf16[640,640]{0,1:T(8,128)(2,1)} %copy.136) | copy-start | bytes 2457604
  71.1 4.7 copy-start.1
  75.8 3.7 copy-start.20
  83.6 3.1 copy-start.25
  86.7 4.7 copy-start.2
  91.4 3.8 copy-start.9
  91.4 3.8 copy-start.19
  96.4 17.2 %copy-start.18 = (f32[640,640]{0,1:T(8,128)}, f32[640,640]{0,1:T(8,128)S(1)}, u32[]{:S(2)}) copy-start(f32[640,640]{0,1:T(8,128)S(1)} %get-tuple-element.124) | copy-start | bytes 4915204
  109.9 3.6 copy-start.55
  118.6 101.4 %reduce-scatter.23.cloned.1.call-start = ((), (), s32[]{:S(2)}) async-start(), calls=%async_computation.18 | async-start | bytes 1228800 | tf_op jit(solution)/shard_map/reduce_scatter | solution.py:288
  121.2 12.6 %slice-start.4 = ((s8[13107200]{0:T(1024)(128)(4,1)}), s8[4194304]{0:T(1024)(128)(4,1)S(1)}, s32[]{:S(2)}) async-start(s8[13107200]{0:T(1024)(128)(4,1)} %bitcast.170), calls=%async_computation.31 | async-start | bytes 8388608
  121.3 12.6 %slice-start.5 = ((s8[13107200]{0:T(1024)(128)(4,1)}), s8[4194304]{0:T(1024)(128)(4,1)S(1)}, s32[]{:S(2)}) async-start(s8[13107200]{0:T(1024)(128)(4,1)} %bitcast.170), calls=%async_computation.32 | async-start | bytes 8388608
  121.3 12.5 %slice-start.6 = ((s8[13107200]{0:T(1024)(128)(4,1)}), s8[4194304]{0:T(1024)(128)(4,1)S(1)}, s32[]{:S(2)}) async-start(s8[13107200]{0:T(1024)(128)(4,1)} %bitcast.170), calls=%async_computation.33 | async-start | bytes 8388608
  121.3 12.5 %slice-start.7 = ((s8[13107200]{0:T(1024)(128)(4,1)}), s8[524288]{0:T(1024)(128)(4,1)S(1)}, s32[]{:S(2)}) async-start(s8[13107200]{0:T(1024)(128)(4,1)} %bitcast.170), calls=%async_computation.34 | async-start | bytes 1048576
  133.8 6.6 copy-start.15
  140.5 3.6 copy-start.10
  146.1 73.9 %reduce-scatter.21.cloned.1.call-start = ((), (), s32[]{:S(2)}) async-start(), calls=%async_computation.17 | async-start | bytes 1228800 | tf_op jit(solution)/shard_map/reduce_scatter | solution.py:288
  146.3 3.2 copy-start.7
  146.3 3.2 copy-start.11
  153.1 66.9 %reduce-scatter.25.cloned.1.call-start = ((), (), s32[]{:S(2)}) async-start(), calls=%async_computation.19 | async-start | bytes 2457600 | tf_op jit(solution)/shard_map/reduce_scatter | solution.py:288
  158.7 7.3 copy-start.37
  158.7 8.2 %copy-start.30 = (bf16[2,640,320]{1,2,0:T(8,128)(2,1)S(1)}, bf16[2,640,320]{1,2,0:T(8,128)(2,1)}, u32[]{:S(2)}) copy-start(bf16[2,640,320]{1,2,0:T(8,128)(2,1)} %copy-done.29) | copy-start | bytes 2457604
  166.9 3.1 copy-start.21
  169.7 50.9 %reduce-scatter.19.cloned.1.call-start = ((), (), s32[]{:S(2)}) async-start(), calls=%async_computation.16 | async-start | bytes 3686400 | tf_op jit(solution)/shard_map/reduce_scatter | solution.py:288
  172.4 12.1 %slice-start = ((s8[13107200]{0:T(1024)(128)(4,1)}), s8[4194304]{0:T(1024)(128)(4,1)S(1)}, s32[]{:S(2)}) async-start(s8[13107200]{0:T(1024)(128)(4,1)} %bitcast.168), calls=%async_computation.27 | async-start | bytes 8388608
  172.4 12.1 %slice-start.1 = ((s8[13107200]{0:T(1024)(128)(4,1)}), s8[4194304]{0:T(1024)(128)(4,1)S(1)}, s32[]{:S(2)}) async-start(s8[13107200]{0:T(1024)(128)(4,1)} %bitcast.168), calls=%async_computation.28 | async-start | bytes 8388608
  172.5 12.9 %slice-start.2 = ((s8[13107200]{0:T(1024)(128)(4,1)}), s8[4194304]{0:T(1024)(128)(4,1)S(1)}, s32[]{:S(2)}) async-start(s8[13107200]{0:T(1024)(128)(4,1)} %bitcast.168), calls=%async_computation.29 | async-start | bytes 8388608
  172.5 13.1 %slice-start.3 = ((s8[13107200]{0:T(1024)(128)(4,1)}), s8[524288]{0:T(1024)(128)(4,1)S(1)}, s32[]{:S(2)}) async-start(s8[13107200]{0:T(1024)(128)(4,1)} %bitcast.168), calls=%async_computation.30 | async-start | bytes 1048576
  185.5 6.6 copy-start.17
  194.3 3.6 copy-start.35
  195.7 3.2 copy-start.32
  202.8 28.7 %reduce-scatter.33.cloned.1.call-start = ((), (), s32[]{:S(2)}) async-start(), calls=%async_computation.23 | async-start | bytes 5898240 | tf_op jit(solution)/shard_map/reduce_scatter | solution.py:288
  211.3 35.5 %reduce-scatter.29.cloned.1.call-start = ((), (), s32[]{:S(2)}) async-start(), calls=%async_computation.21 | async-start | bytes 5898240 | tf_op jit(solution)/shard_map/reduce_scatter | solution.py:288
  219.8 162.3 %all-reduce.7.cloned.1.call-start = ((), (), s32[]{:S(2)}) async-start(), calls=%async_computation.26 | async-start | bytes 4096000
  220.6 241.9 %reduce-scatter.35.cloned.1.call-start = ((), (), s32[]{:S(2)}) async-start(), calls=%async_computation.24 | async-start | bytes 1392640
  223.2 368.8 %reduce-scatter.37.cloned.1.call-start = ((), (), s32[]{:S(2)}) async-start(), calls=%async_computation.25 | async-start | bytes 2506752
  235.6 488.2 %reduce-scatter.31.cloned.1.call-start = ((), (), s32[]{:S(2)}) async-start(), calls=%async_computation.22 | async-start | bytes 2088960 | tf_op jit(solution)/shard_map/reduce_scatter | solution.py:290
  249.6 5.1 copy-start.38
  249.6 9.3 %all-to-all-start.2 = ((f32[2,640,320]{1,2,0:T(8,128)}), f32[2,640,320]{1,2,0:T(8,128)}, u32[]{:S(2)}, u32[]{:S(2)}) async-start(f32[2,640,320]{1,2,0:T(8,128)} %pad_maximum_fusion.1), calls=%async_computation.2 | async-start | bytes 3276800 | tf_op jit(solution)/shard_map/all_to_all | solution.py:55
  258.9 14.0 %all-to-all-start.5 = ((bf16[2,640,320]{1,2,0:T(8,128)(2,1)}), bf16[2,640,320]{1,2,0:T(8,128)(2,1)S(1)}, u32[]{:S(2)}, u32[]{:S(2)}) async-start(bf16[2,640,320]{1,2,0:T(8,128)(2,1)} %pad_maximum_fusion.8), calls=%async_computation.5 | async-start | bytes 1638400 | tf_op jit(solution)/shard_map/all_to_all | solution.py:55
  262.4 2.9 copy-start.27
  262.4 2.9 copy-start.36
  262.4 2.9 copy-start.41
  262.5 2.9 copy-start.43
  262.5 2.9 copy-start.45
  262.5 2.9 copy-start.47
  265.4 4.1 copy-start.5
  272.9 7.3 all-to-all-start.4
  279.0 4.0 copy-start.54
  (17 other events, 30.7 us)
Sparse Core Ops, SparseCore 0:
  118.7 11.1 reduce-scatter.26
  146.2 11.1 reduce-scatter.22
  159.7 9.4 reduce-scatter.20
  171.9 10.2 reduce-scatter.24
  202.9 13.2 reduce-scatter.18
  218.4 13.0 reduce-scatter.32
  233.7 13.0 reduce-scatter.28
  253.8 128.3 all-reduce.6
  384.5 77.9 reduce-scatter.34
  467.2 124.7 reduce-scatter.36
  597.7 126.0 reduce-scatter.30
